TPU v7x, 32 devices: a whole 2x2x4 slice. The times are simulated.
32 devices in a mesh: layer: 8 (over y, x, core), batch: 4 (over z).
Axes of the slice: x: 2, y: 2, z: 4, core: 2. Of those that a mesh axis runs over, the one named last changes fastest.
Arguments:
- images: bfloat16 [32, 4, 4, 512], P('batch'), parts along dimension 0, may hold values from -6 to 6
- weights: bfloat16 [16, 4608, 512], P('layer'), may hold values from -0.25 to 0.25
- biases: float32 [16, 512], P('layer'), may hold values from -3 to 3
Outputs:
- states: float32 [16, 32, 4, 4, 512], P('layer', 'batch'), parts along dimension 1
There are 4 independent parts, one for each index of `batch`. A program takes and returns all parts, laid end to end along the dimension named above; an argument that names none is the same for every part. Nothing has to cross between parts.
All inputs are finite; a program needn't handle non-finite values.
Results may differ from a plain program's by a relative error of at most 0.015.
Values sent between devices are 32-bit elements; how exact they have to be, the bound alone decides.
A program may use at most 64 MiB of HBM per device.

v0:
```python
import functools

import jax
import jax.numpy as jnp
from jax import lax
from jax.experimental import pallas as pl
from jax.experimental.pallas import tpu as pltpu
from jax.sharding import PartitionSpec as P

MESH = pl.DeviceIdType.MESH
step_size = 0.25


def dot(a, b):
    return jnp.dot(a, b, preferred_element_type=jnp.float32)


def kernel(
    n,
    img_ref,
    w_hbm,
    b_ref,
    out_ref,
    wv,
    pad,
    cols,
    gsend,
    shifted,
    stage,
    force,
    wsend,
    wrecv,
    wc,
    bc,
    fo,
    cin,
    abuf,
    bbuf,
    peer_fin,
    peer_out,
    w_sem,
    g_sem,
    wx_sem,
    fx_sem,
    cs_sem,
    cr_sem,
    pf_sem,
    po_sem,
):
    me = lax.axis_index("layer")
    right, left = lax.rem(me + 1, n), lax.rem(me + n - 1, n)
    images, side, _, channels = img_ref.shape
    half = channels // 2
    rows = side * side * images
    has_next = me < n - 1
    has_next_pair = me < n - 2
    core = lax.rem(me, 2)
    other = 1 - core
    partner = me + 1 - 2 * core
    ahead, behind = lax.rem(me + 2, n), lax.rem(me + n - 2, n)
    groups = side // 2

    def loads(l, h):
        return [
            pltpu.make_async_copy(
                w_hbm.at[l, 3 * r : 3 * r + 3, h],
                wv.at[l, 3 * r : 3 * r + 3, h],
                w_sem.at[l, h, r],
            )
            for r in range(3)
        ]

    def start_load(l, h):
        for copy in loads(l, h):
            copy.start()

    def wait_load(l, h):
        for copy in loads(l, h):
            copy.wait()

    start_load(0, 0)
    start_load(0, 1)

    barrier = pltpu.get_barrier_semaphore()
    for neighbour in (left, right, behind, ahead):
        pl.semaphore_signal(
            barrier, inc=1, device_id={"layer": neighbour}, device_id_type=MESH
        )

    def remote(src, dst, send_sem, recv_sem, target):
        return pltpu.make_async_remote_copy(
            src_ref=src,
            dst_ref=dst,
            send_sem=send_sem,
            recv_sem=recv_sem,
            device_id={"layer": target},
            device_id_type=MESH,
        )

    def send_guess(q):
        return remote(gsend.at[q], shifted.at[q], g_sem.at[0, q], g_sem.at[1, q], right)

    def send_centre():
        return remote(wsend, wrecv, wx_sem.at[0], wx_sem.at[1], partner)

    def send_force():
        away = force.at[pl.ds(groups * other, groups)]
        return remote(away, fo.at[core], fx_sem.at[0], fx_sem.at[1], partner)

    def first_coarse(t, g):
        src = out_ref.at[1, groups * t + g]
        return remote(src, cin.at[g], cs_sem.at[t, g], cr_sem.at[g], me + 1 + t)

    def send_coarse(g):
        return remote(bbuf.at[g], cin.at[g], cs_sem.at[0, g], cr_sem.at[g], ahead)

    def send_fin(src, g):
        return remote(src.at[g], peer_fin.at[g], pf_sem.at[0, g], pf_sem.at[1, g], partner)

    def send_out(src, g):
        return remote(src.at[g], peer_out.at[g], po_sem.at[0, g], po_sem.at[1, g], partner)

    def cut(h):
        return slice(h * half, (h + 1) * half)

    def build(h):
        for tap in range(9):
            dy, dx = tap // 3, tap % 3
            piece = pad[dy : dy + side, dx : dx + side, :, cut(h)]
            cols[h, :, tap * half : (tap + 1) * half] = piece.reshape(rows, half).astype(
                jnp.bfloat16
            )

    def weight(l, h, q):
        return wv[l, :, h, :, cut(q)].reshape(9 * half, half)

    def fine(l, before, emit):
        before(0)
        build(0)
        parts = [dot(cols[0], weight(l, 0, q)) for q in range(2)]
        before(1)
        build(1)
        for q in range(2):
            mixed = parts[q] + dot(cols[1], weight(l, 1, q)) + b_ref[l : l + 1, cut(q)]
            base = pad[1 : 1 + side, 1 : 1 + side, :, cut(q)].reshape(rows, half)
            emit(q, base + step_size * jnp.tanh(mixed))

    def grid_of(value):
        return value.reshape(side, side, images, value.shape[-1])

    def to_pad(q, value):
        pad[1 : 1 + side, 1 : 1 + side, :, cut(q)] = grid_of(value)

    def coarse(field, centre, bias):
        mixed = dot(field.astype(jnp.bfloat16), centre) + bias
        return field + 2.0 * step_size * jnp.tanh(mixed)

    def no_wait(h):
        pass

    pad[...] = jnp.zeros_like(pad)
    lanes = 128
    tiles = channels // lanes
    for m in range(images):
        for i in range(side):
            row = img_ref[m, i].astype(jnp.float32)
            for c in range(tiles):
                at = ((m * side + i) * tiles + c) * side
                stage[at : at + side, :] = row[:, c * lanes : (c + 1) * lanes]
    for i in range(side):
        for c in range(tiles):
            for j in range(side):
                at = (i * tiles + c) * side + j
                pad[1 + i, 1 + j, :, c * lanes : (c + 1) * lanes] = stage[
                    pl.ds(at, images, stride=side * tiles * side), :
                ]

    def first_layer(h):
        wait_load(0, h)
        start_load(1, h)

    fine(0, first_layer, to_pad)

    @pl.when(me == 0)
    def _():
        out_ref[0] = pad[1 : 1 + side, 1 : 1 + side]

    pl.semaphore_wait(barrier, 4)

    @pl.when(me >= 2)
    def _():
        centre = wv[0, 4].reshape(channels, channels)
        wsend[0:channels, :] = centre.astype(jnp.float32)
        wsend[channels : channels + 8, :] = jnp.broadcast_to(b_ref[0:1, :], (8, channels))
        send_centre().start()
        wc[core] = centre
        bc[core] = jnp.broadcast_to(b_ref[0:1, :], (8, channels))

    def emit_guess(q, value):
        gsend[q] = value

        @pl.when(has_next)
        def _():
            send_guess(q).start()

    fine(1, lambda h: wait_load(1, h), emit_guess)

    @pl.when(me == 0)
    def _():
        for q in range(2):
            out_ref[1, :, :, :, cut(q)] = grid_of(gsend[q])

    @pl.when(me >= 1)
    def _():
        def arrive(h):
            send_guess(h).wait_recv()
            to_pad(h, shifted[h])

        fine(0, arrive, to_pad)

        @pl.when(me == 1)
        def _():
            out_ref[0] = pad[1 : 1 + side, 1 : 1 + side]

        def emit_end(q, value):
            out_ref[1, :, :, :, cut(q)] = grid_of(value)

        fine(1, no_wait, emit_end)

        @pl.when((me == 1) & has_next_pair)
        def _():
            for g in range(groups):
                for t in range(2):
                    first_coarse(t, g).start()

    @pl.when(me >= 2)
    def _():
        start = jnp.concatenate([shifted[0], shifted[1]], axis=1)
        centre = wv[0, 4].reshape(channels, channels)
        force[...] = out_ref[1] - grid_of(coarse(start, centre, b_ref[0:1, :]))
        send_force().start()
        fo[core] = force[pl.ds(groups * core, groups)]
        send_centre().wait_recv()
        wc[other] = wrecv[0:channels, :].astype(jnp.bfloat16)
        bc[other] = wrecv[channels : channels + 8, :]
        send_force().wait_recv()

        def advance(field, b, g):
            flat = field.reshape(side * images, channels)
            solved = coarse(flat, wc[b], bc[b, 0:1, :])
            return solved.reshape(side, images, channels) + fo[b, g]

        for g in range(groups):
            send_coarse(g).wait_recv()

            @pl.when(core == 1)
            def _():
                send_fin(cin, g).start()

            field = cin[g]
            first = advance(field, 0, g)
            abuf[g] = first

            @pl.when(core == 0)
            def _():
                send_fin(abuf, g).start()

            second = advance(first, 1, g)
            bbuf[g] = second

            @pl.when(has_next_pair)
            def _():
                send_coarse(g).start()

            @pl.when(core == 0)
            def _():
                send_out(bbuf, g).start()

            @pl.when(core == 1)
            def _():
                send_out(abuf, g).start()

            own = groups * core + g
            pad[1 + own, 1 : 1 + side] = jnp.where(core == 0, field, first)
            out_ref[1, own] = jnp.where(core == 0, first, second)

        for g in range(groups):
            send_fin(cin, g).wait_recv()
            pad[1 + groups * other + g, 1 : 1 + side] = peer_fin[g]

        def emit_finished(q, value):
            out_ref[0, :, :, :, cut(q)] = grid_of(value)

        fine(0, no_wait, emit_finished)
        for g in range(groups):
            send_out(abuf, g).wait_recv()
            out_ref[1, groups * other + g] = peer_out[g]

        send_centre().wait_send()
        send_force().wait_send()
        for g in range(groups):
            send_fin(cin, g).wait_send()
            send_out(abuf, g).wait_send()

            @pl.when(has_next_pair)
            def _():
                send_coarse(g).wait_send()

    @pl.when(has_next)
    def _():
        for q in range(2):
            send_guess(q).wait_send()

    @pl.when((me == 1) & has_next_pair)
    def _():
        for g in range(groups):
            for t in range(2):
                first_coarse(t, g).wait_send()


def shards(n, images, weights, biases):
    count, side, _, channels = images.shape
    half = channels // 2
    rows = side * side * count
    groups = side // 2
    piece = (groups, side, count, channels)
    taps = weights.reshape(2, 9, 2, half, channels)
    vmem = pl.BlockSpec(memory_space=pltpu.VMEM)
    f32, bf16 = jnp.float32, jnp.bfloat16
    out = pl.pallas_call(
        functools.partial(kernel, n),
        out_shape=jax.ShapeDtypeStruct((2, side, side, count, channels), f32),
        in_specs=[vmem, pl.BlockSpec(memory_space=pl.ANY), vmem],
        out_specs=vmem,
        scratch_shapes=[
            pltpu.VMEM(taps.shape, bf16),
            pltpu.VMEM((side + 2, side + 2, count, channels), f32),
            pltpu.VMEM((2, rows, 9 * half), bf16),
            pltpu.VMEM((2, rows, half), f32),
            pltpu.VMEM((2, rows, half), f32),
            pltpu.VMEM((rows * channels // 128, 128), f32),
            pltpu.VMEM((side, side, count, channels), f32),
            pltpu.VMEM((channels + 8, channels), f32),
            pltpu.VMEM((channels + 8, channels), f32),
            pltpu.VMEM((2, channels, channels), bf16),
            pltpu.VMEM((2, 8, channels), f32),
            pltpu.VMEM((2,) + piece, f32),
            pltpu.VMEM(piece, f32),
            pltpu.VMEM(piece, f32),
            pltpu.VMEM(piece, f32),
            pltpu.VMEM(piece, f32),
            pltpu.VMEM(piece, f32),
            pltpu.SemaphoreType.DMA((2, 2, 3)),
            pltpu.SemaphoreType.DMA((2, 2)),
            pltpu.SemaphoreType.DMA((2,)),
            pltpu.SemaphoreType.DMA((2,)),
            pltpu.SemaphoreType.DMA((2, groups)),
            pltpu.SemaphoreType.DMA((groups,)),
            pltpu.SemaphoreType.DMA((2, groups)),
            pltpu.SemaphoreType.DMA((2, groups)),
        ],
        compiler_params=pltpu.CompilerParams(
            collective_id=0, has_side_effects=True, vmem_limit_bytes=56 * 2**20
        ),
    )(images, taps, biases)
    return jnp.transpose(out, (0, 3, 1, 2, 4))


def solution(mesh):
    return jax.shard_map(
        functools.partial(shards, mesh.shape["layer"]),
        mesh=mesh,
        in_specs=(P("batch", None, None, None), P("layer", None, None), P("layer", None)),
        out_specs=P("layer", "batch", None, None, None),
        check_vma=False,
    )
```

profile of v0, /device:TPU:15, one launch (start us, length us, event | category | flops | bytes accessed | tf_op | source)
XLA Modules:
  0.0 27.0 jit_solution(8868286623680475987)
XLA Ops:
  0.0 24.8 %shard_map.37 = f32[2,4,4,8,512]{4,3,2,1,0:T(8,128)} custom-call(bf16[8,4,4,512]{3,2,1,0:T(4,128)(2,1)} %img_ref.1, bf16[2,9,2,256,512]{4,3,2,1,0:T(8,128)(2,1)} %bitcast.2, f32[2,512]{1,0:T(2,128)} %b_ref.1), custom_call_target="tpu_custom_call" | custom-call | tf_op jit(solution)/shard_map/pallas_call | solution.py:330
  24.8 2.2 %copy.4 = f32[2,8,4,4,512]{4,3,2,1,0:T(4,128)} copy(f32[2,8,4,4,512]{4,1,3,2,0:T(8,128)} %bitcast.3) | data formatting | bytes 1048576 | tf_op jit(solution)/shard_map/transpose | solution.py:366
where the time goes:
time: 27.2 us; the launch traced here: 27 us
  Pallas kernels  24.8 us (91%)
  local copies, waits for them, and re-layouts  2.17 us (8%)
    pallas_call x1, Pallas kernels, shards(): pl.pallas_call(functools.partial(kernel, n), out_shape=jax.ShapeDtypeStru...  24.8 us
    transpose x1, local copies, waits for them, and re-layouts, shards(): return jnp.transpose(out, (0, 3, 1, 2, 4))  2.17 us

commit v1 on v0

--- a/solution.py
+++ b/solution.py
@@ -17,10 +17,12 @@
 
 def kernel(
     n,
+    img_hbm,
+    w_hbm,
+    b_hbm,
+    out_ref,
     img_ref,
-    w_hbm,
     b_ref,
-    out_ref,
     wv,
     pad,
     cols,
@@ -38,6 +40,7 @@
     bbuf,
     peer_fin,
     peer_out,
+    in_sem,
     w_sem,
     g_sem,
     wx_sem,
@@ -78,6 +81,10 @@
         for copy in loads(l, h):
             copy.wait()
 
+    get_images = pltpu.make_async_copy(img_hbm, img_ref, in_sem.at[0])
+    get_biases = pltpu.make_async_copy(b_hbm, b_ref, in_sem.at[1])
+    get_images.start()
+    get_biases.start()
     start_load(0, 0)
     start_load(0, 1)
 
@@ -159,6 +166,8 @@
         pass
 
     pad[...] = jnp.zeros_like(pad)
+    get_images.wait()
+    get_biases.wait()
     lanes = 128
     tiles = channels // lanes
     for m in range(images):
@@ -326,13 +335,16 @@
     piece = (groups, side, count, channels)
     taps = weights.reshape(2, 9, 2, half, channels)
     vmem = pl.BlockSpec(memory_space=pltpu.VMEM)
+    hbm = pl.BlockSpec(memory_space=pl.ANY)
     f32, bf16 = jnp.float32, jnp.bfloat16
     out = pl.pallas_call(
         functools.partial(kernel, n),
-        out_shape=jax.ShapeDtypeStruct((2, side, side, count, channels), f32),
-        in_specs=[vmem, pl.BlockSpec(memory_space=pl.ANY), vmem],
+        out_shape=pltpu.VMEM((2, side, side, count, channels), f32),
+        in_specs=[hbm, hbm, hbm],
         out_specs=vmem,
         scratch_shapes=[
+            pltpu.VMEM(images.shape, bf16),
+            pltpu.VMEM(biases.shape, f32),
             pltpu.VMEM(taps.shape, bf16),
             pltpu.VMEM((side + 2, side + 2, count, channels), f32),
             pltpu.VMEM((2, rows, 9 * half), bf16),
@@ -350,6 +362,7 @@
             pltpu.VMEM(piece, f32),
             pltpu.VMEM(piece, f32),
             pltpu.VMEM(piece, f32),
+            pltpu.SemaphoreType.DMA((2,)),
             pltpu.SemaphoreType.DMA((2, 2, 3)),
             pltpu.SemaphoreType.DMA((2, 2)),
             pltpu.SemaphoreType.DMA((2,)),

time: 27.2 us -> 25 us (0.919)
  Pallas kernels: 24.8 us -> 23.7 us
  local copies, waits for them, and re-layouts: 2.17 us -> 1.13 us
    pallas_call x1, Pallas kernels: 24.8 us -> 23.7 us  [shards(): pl.pallas_call(functools.partial(kernel, n), out_shape=pltpu.VMEM((2, sid...]
    transpose x1, local copies, waits for them, and re-layouts: 2.17 us -> 1.13 us  [shards(): return jnp.transpose(out, (0, 3, 1, 2, 4))]
where the time goes in v1:
time: 25 us; the launch traced here: 24.8 us
  Pallas kernels  23.7 us (95%)
  local copies, waits for them, and re-layouts  1.13 us (5%)
    pallas_call x1, Pallas kernels, shards(): pl.pallas_call(functools.partial(kernel, n), out_shape=pltpu.VMEM((2, sid...  23.7 us
    transpose x1, local copies, waits for them, and re-layouts, shards(): return jnp.transpose(out, (0, 3, 1, 2, 4))  1.13 us

profile of v1, /device:TPU:15, one launch (start us, length us, event | category | flops | bytes accessed | tf_op | source)
XLA Modules:
  0.0 24.8 jit_solution(4378738217468366148)
XLA Ops:
  0.0 23.7 %shard_map.37 = f32[2,4,4,8,512]{4,3,2,1,0:T(8,128)S(1)} custom-call(bf16[8,4,4,512]{3,2,1,0:T(4,128)(2,1)} %img_hbm.1, bf16[2,9,2,256,512]{4,3,2,1,0:T(8,128)(2,1)} %bitcast.3, f32[2,512]{1,0:T(2,128)} %b_hbm.1), custom_call_target="tpu_custom_call" | custom-call | tf_op jit(solution)/shard_map/pallas_call | solution.py:340
  23.7 1.1 %copy.4 = f32[2,8,4,4,512]{4,3,2,1,0:T(4,128)} copy(f32[2,8,4,4,512]{4,1,3,2,0:T(8,128)S(1)} %bitcast.2) | data formatting | bytes 1048576 | tf_op jit(solution)/shard_map/transpose | solution.py:379

commit v2 on v1

--- a/solution.py
+++ b/solution.py
@@ -51,7 +51,7 @@
     po_sem,
 ):
     me = lax.axis_index("layer")
-    right, left = lax.rem(me + 1, n), lax.rem(me + n - 1, n)
+    right = lax.rem(me + 1, n)
     images, side, _, channels = img_ref.shape
     half = channels // 2
     rows = side * side * images
@@ -60,8 +60,10 @@
     core = lax.rem(me, 2)
     other = 1 - core
     partner = me + 1 - 2 * core
-    ahead, behind = lax.rem(me + 2, n), lax.rem(me + n - 2, n)
-    groups = side // 2
+    runs = (me >= 2) & (core == jnp.where(has_next_pair, 0, 1))
+    helps = (me >= 2) & (core == jnp.where(has_next_pair, 1, 0))
+    runner_ahead = jnp.where(me == n - 4, n - 1, lax.rem(me + 2, n))
+    groups = side
 
     def loads(l, h):
         return [
@@ -89,7 +91,8 @@
     start_load(0, 1)
 
     barrier = pltpu.get_barrier_semaphore()
-    for neighbour in (left, right, behind, ahead):
+    for distance in (1, 2, 3, n - 3, n - 2, n - 1):
+        neighbour = lax.rem(me + distance, n)
         pl.semaphore_signal(
             barrier, inc=1, device_id={"layer": neighbour}, device_id_type=MESH
         )
@@ -111,15 +114,14 @@
         return remote(wsend, wrecv, wx_sem.at[0], wx_sem.at[1], partner)
 
     def send_force():
-        away = force.at[pl.ds(groups * other, groups)]
-        return remote(away, fo.at[core], fx_sem.at[0], fx_sem.at[1], partner)
-
-    def first_coarse(t, g):
-        src = out_ref.at[1, groups * t + g]
-        return remote(src, cin.at[g], cs_sem.at[t, g], cr_sem.at[g], me + 1 + t)
+        return remote(force, fo.at[core], fx_sem.at[0], fx_sem.at[1], partner)
+
+    def first_coarse(g):
+        src = out_ref.at[1, g]
+        return remote(src, cin.at[g], cs_sem.at[g], cr_sem.at[g], 2 if n > 4 else n - 1)
 
     def send_coarse(g):
-        return remote(bbuf.at[g], cin.at[g], cs_sem.at[0, g], cr_sem.at[g], ahead)
+        return remote(bbuf.at[g], cin.at[g], cs_sem.at[g], cr_sem.at[g], runner_ahead)
 
     def send_fin(src, g):
         return remote(src.at[g], peer_fin.at[g], pf_sem.at[0, g], pf_sem.at[1, g], partner)
@@ -194,15 +196,18 @@
     def _():
         out_ref[0] = pad[1 : 1 + side, 1 : 1 + side]
 
-    pl.semaphore_wait(barrier, 4)
-
-    @pl.when(me >= 2)
+    pl.semaphore_wait(barrier, 6)
+
+    @pl.when(helps)
     def _():
         centre = wv[0, 4].reshape(channels, channels)
         wsend[0:channels, :] = centre.astype(jnp.float32)
         wsend[channels : channels + 8, :] = jnp.broadcast_to(b_ref[0:1, :], (8, channels))
         send_centre().start()
-        wc[core] = centre
+
+    @pl.when(runs)
+    def _():
+        wc[core] = wv[0, 4].reshape(channels, channels)
         bc[core] = jnp.broadcast_to(b_ref[0:1, :], (8, channels))
 
     def emit_guess(q, value):
@@ -239,16 +244,19 @@
         @pl.when((me == 1) & has_next_pair)
         def _():
             for g in range(groups):
-                for t in range(2):
-                    first_coarse(t, g).start()
-
-    @pl.when(me >= 2)
-    def _():
+                first_coarse(g).start()
+
+    def own_forcing():
         start = jnp.concatenate([shifted[0], shifted[1]], axis=1)
         centre = wv[0, 4].reshape(channels, channels)
-        force[...] = out_ref[1] - grid_of(coarse(start, centre, b_ref[0:1, :]))
-        send_force().start()
-        fo[core] = force[pl.ds(groups * core, groups)]
+        return out_ref[1] - grid_of(coarse(start, centre, b_ref[0:1, :]))
+
+    def emit_finished(q, value):
+        out_ref[0, :, :, :, cut(q)] = grid_of(value)
+
+    @pl.when(runs)
+    def _():
+        fo[core] = own_forcing()
         send_centre().wait_recv()
         wc[other] = wrecv[0:channels, :].astype(jnp.bfloat16)
         bc[other] = wrecv[channels : channels + 8, :]
@@ -269,44 +277,23 @@
             field = cin[g]
             first = advance(field, 0, g)
             abuf[g] = first
-
-            @pl.when(core == 0)
-            def _():
-                send_fin(abuf, g).start()
-
             second = advance(first, 1, g)
             bbuf[g] = second
 
             @pl.when(has_next_pair)
             def _():
                 send_coarse(g).start()
-
-            @pl.when(core == 0)
-            def _():
+                send_fin(abuf, g).start()
                 send_out(bbuf, g).start()
 
             @pl.when(core == 1)
             def _():
                 send_out(abuf, g).start()
 
-            own = groups * core + g
-            pad[1 + own, 1 : 1 + side] = jnp.where(core == 0, field, first)
-            out_ref[1, own] = jnp.where(core == 0, first, second)
-
-        for g in range(groups):
-            send_fin(cin, g).wait_recv()
-            pad[1 + groups * other + g, 1 : 1 + side] = peer_fin[g]
-
-        def emit_finished(q, value):
-            out_ref[0, :, :, :, cut(q)] = grid_of(value)
+            pad[1 + g, 1 : 1 + side] = jnp.where(core == 0, field, first)
+            out_ref[1, g] = jnp.where(core == 0, first, second)
 
         fine(0, no_wait, emit_finished)
-        for g in range(groups):
-            send_out(abuf, g).wait_recv()
-            out_ref[1, groups * other + g] = peer_out[g]
-
-        send_centre().wait_send()
-        send_force().wait_send()
         for g in range(groups):
             send_fin(cin, g).wait_send()
             send_out(abuf, g).wait_send()
@@ -315,6 +302,20 @@
             def _():
                 send_coarse(g).wait_send()
 
+    @pl.when(helps)
+    def _():
+        force[...] = own_forcing()
+        send_force().start()
+        for g in range(groups):
+            send_fin(cin, g).wait_recv()
+            pad[1 + g, 1 : 1 + side] = peer_fin[g]
+        fine(0, no_wait, emit_finished)
+        for g in range(groups):
+            send_out(abuf, g).wait_recv()
+            out_ref[1, g] = peer_out[g]
+        send_centre().wait_send()
+        send_force().wait_send()
+
     @pl.when(has_next)
     def _():
         for q in range(2):
@@ -323,15 +324,14 @@
     @pl.when((me == 1) & has_next_pair)
     def _():
         for g in range(groups):
-            for t in range(2):
-                first_coarse(t, g).wait_send()
+            first_coarse(g).wait_send()
 
 
 def shards(n, images, weights, biases):
     count, side, _, channels = images.shape
     half = channels // 2
     rows = side * side * count
-    groups = side // 2
+    groups = side
     piece = (groups, side, count, channels)
     taps = weights.reshape(2, 9, 2, half, channels)
     vmem = pl.BlockSpec(memory_space=pltpu.VMEM)
@@ -367,7 +367,7 @@
             pltpu.SemaphoreType.DMA((2, 2)),
             pltpu.SemaphoreType.DMA((2,)),
             pltpu.SemaphoreType.DMA((2,)),
-            pltpu.SemaphoreType.DMA((2, groups)),
+            pltpu.SemaphoreType.DMA((groups,)),
             pltpu.SemaphoreType.DMA((groups,)),
             pltpu.SemaphoreType.DMA((2, groups)),
             pltpu.SemaphoreType.DMA((2, groups)),

time: 25 us -> 23.8 us (0.952)
  Pallas kernels: 23.7 us -> 22.4 us
    pallas_call x1, Pallas kernels: 23.7 us -> 22.4 us  [shards(): pl.pallas_call(functools.partial(kernel, n), out_shape=pltpu.VMEM((2, sid...]
where the time goes in v2:
time: 23.8 us; the launch traced here: 23.5 us
  Pallas kernels  22.4 us (94%)
  local copies, waits for them, and re-layouts  1.13 us (5%)
    pallas_call x1, Pallas kernels, shards(): pl.pallas_call(functools.partial(kernel, n), out_shape=pltpu.VMEM((2, sid...  22.4 us
    transpose x1, local copies, waits for them, and re-layouts, shards(): return jnp.transpose(out, (0, 3, 1, 2, 4))  1.13 us

profile of v2, /device:TPU:15, one launch (start us, length us, event | category | flops | bytes accessed | tf_op | source)
XLA Modules:
  0.0 23.5 jit_solution(6402239588955138158)
XLA Ops:
  0.0 22.4 %shard_map.37 = f32[2,4,4,8,512]{4,3,2,1,0:T(8,128)S(1)} custom-call(bf16[8,4,4,512]{3,2,1,0:T(4,128)(2,1)} %img_hbm.1, bf16[2,9,2,256,512]{4,3,2,1,0:T(8,128)(2,1)} %bitcast.3, f32[2,512]{1,0:T(2,128)} %b_hbm.1), custom_call_target="tpu_custom_call" | custom-call | tf_op jit(solution)/shard_map/pallas_call | solution.py:340
  22.4 1.1 %copy.4 = f32[2,8,4,4,512]{4,3,2,1,0:T(4,128)} copy(f32[2,8,4,4,512]{4,1,3,2,0:T(8,128)S(1)} %bitcast.2) | data formatting | bytes 1048576 | tf_op jit(solution)/shard_map/transpose | solution.py:379

commit v3 on v2

--- a/solution.py
+++ b/solution.py
@@ -29,6 +29,7 @@
     gsend,
     shifted,
     stage,
+    centre_dot,
     force,
     wsend,
     wrecv,
@@ -132,25 +133,32 @@
     def cut(h):
         return slice(h * half, (h + 1) * half)
 
+    band = side * images
+
     def build(h):
-        for tap in range(9):
-            dy, dx = tap // 3, tap % 3
-            piece = pad[dy : dy + side, dx : dx + side, :, cut(h)]
-            cols[h, :, tap * half : (tap + 1) * half] = piece.reshape(rows, half).astype(
-                jnp.bfloat16
-            )
-
-    def weight(l, h, q):
-        return wv[l, :, h, :, cut(q)].reshape(9 * half, half)
+        for dx in range(3):
+            piece = pad[1 : 1 + side, dx : dx + side, :, cut(h)]
+            cols[h, band : band + rows, dx * half : (dx + 1) * half] = piece.reshape(
+                rows, half
+            ).astype(jnp.bfloat16)
+
+    def taps_of(l, h, q):
+        total = None
+        for dy in range(3):
+            window = cols[h, dy * band : dy * band + rows, :]
+            block = wv[l, 3 * dy : 3 * dy + 3, h, :, cut(q)].reshape(3 * half, half)
+            part = dot(window, block)
+            total = part if total is None else total + part
+        return total
 
     def fine(l, before, emit):
         before(0)
         build(0)
-        parts = [dot(cols[0], weight(l, 0, q)) for q in range(2)]
+        parts = [taps_of(l, 0, q) for q in range(2)]
         before(1)
         build(1)
         for q in range(2):
-            mixed = parts[q] + dot(cols[1], weight(l, 1, q)) + b_ref[l : l + 1, cut(q)]
+            mixed = parts[q] + taps_of(l, 1, q) + b_ref[l : l + 1, cut(q)]
             base = pad[1 : 1 + side, 1 : 1 + side, :, cut(q)].reshape(rows, half)
             emit(q, base + step_size * jnp.tanh(mixed))
 
@@ -168,6 +176,9 @@
         pass
 
     pad[...] = jnp.zeros_like(pad)
+    for h in range(2):
+        cols[h, 0:band, :] = jnp.zeros((band, 3 * half), jnp.bfloat16)
+        cols[h, band + rows :, :] = jnp.zeros((band, 3 * half), jnp.bfloat16)
     get_images.wait()
     get_biases.wait()
     lanes = 128
@@ -227,6 +238,20 @@
     @pl.when(me >= 1)
     def _():
         def arrive(h):
+            if h == 0:
+
+                @pl.when(runs)
+                def _():
+                    send_centre().wait_recv()
+                    wc[other] = wrecv[0:channels, :].astype(jnp.bfloat16)
+                    bc[other] = wrecv[channels : channels + 8, :]
+
+            else:
+
+                @pl.when(me >= 2)
+                def _():
+                    centre_dot[...] = dot(shifted[0].astype(jnp.bfloat16), wv[0, 4, 0])
+
             send_guess(h).wait_recv()
             to_pad(h, shifted[h])
 
@@ -248,8 +273,9 @@
 
     def own_forcing():
         start = jnp.concatenate([shifted[0], shifted[1]], axis=1)
-        centre = wv[0, 4].reshape(channels, channels)
-        return out_ref[1] - grid_of(coarse(start, centre, b_ref[0:1, :]))
+        rest = dot(shifted[1].astype(jnp.bfloat16), wv[0, 4, 1])
+        mixed = centre_dot[...] + rest + b_ref[0:1, :]
+        return out_ref[1] - grid_of(start + 2.0 * step_size * jnp.tanh(mixed))
 
     def emit_finished(q, value):
         out_ref[0, :, :, :, cut(q)] = grid_of(value)
@@ -257,9 +283,6 @@
     @pl.when(runs)
     def _():
         fo[core] = own_forcing()
-        send_centre().wait_recv()
-        wc[other] = wrecv[0:channels, :].astype(jnp.bfloat16)
-        bc[other] = wrecv[channels : channels + 8, :]
         send_force().wait_recv()
 
         def advance(field, b, g):
@@ -347,10 +370,11 @@
             pltpu.VMEM(biases.shape, f32),
             pltpu.VMEM(taps.shape, bf16),
             pltpu.VMEM((side + 2, side + 2, count, channels), f32),
-            pltpu.VMEM((2, rows, 9 * half), bf16),
+            pltpu.VMEM((2, rows + 2 * side * count, 3 * half), bf16),
             pltpu.VMEM((2, rows, half), f32),
             pltpu.VMEM((2, rows, half), f32),
             pltpu.VMEM((rows * channels // 128, 128), f32),
+            pltpu.VMEM((rows, channels), f32),
             pltpu.VMEM((side, side, count, channels), f32),
             pltpu.VMEM((channels + 8, channels), f32),
             pltpu.VMEM((channels + 8, channels), f32),

time: 23.8 us -> 23.1 us (0.971)
  Pallas kernels: 22.4 us -> 21.7 us
    pallas_call x1, Pallas kernels: 22.4 us -> 21.7 us  [shards(): pl.pallas_call(functools.partial(kernel, n), out_shape=pltpu.VMEM((2, sid...]
where the time goes in v3:
time: 23.1 us; the launch traced here: 22.9 us
  Pallas kernels  21.7 us (94%)
  local copies, waits for them, and re-layouts  1.13 us (5%)
    pallas_call x1, Pallas kernels, shards(): pl.pallas_call(functools.partial(kernel, n), out_shape=pltpu.VMEM((2, sid...  21.7 us
    transpose x1, local copies, waits for them, and re-layouts, shards(): return jnp.transpose(out, (0, 3, 1, 2, 4))  1.13 us

profile of v3, /device:TPU:15, one launch (start us, length us, event | category | flops | bytes accessed | tf_op | source)
XLA Modules:
  0.0 22.9 jit_solution(9103339409473105975)
XLA Ops:
  0.0 21.7 %shard_map.37 = f32[2,4,4,8,512]{4,3,2,1,0:T(8,128)S(1)} custom-call(bf16[8,4,4,512]{3,2,1,0:T(4,128)(2,1)} %img_hbm.1, bf16[2,9,2,256,512]{4,3,2,1,0:T(8,128)(2,1)} %bitcast.3, f32[2,512]{1,0:T(2,128)} %b_hbm.1), custom_call_target="tpu_custom_call" | custom-call | tf_op jit(solution)/shard_map/pallas_call | solution.py:363
  21.7 1.1 %copy.4 = f32[2,8,4,4,512]{4,3,2,1,0:T(4,128)} copy(f32[2,8,4,4,512]{4,1,3,2,0:T(8,128)S(1)} %bitcast.2) | data formatting | bytes 1048576 | tf_op jit(solution)/shard_map/transpose | solution.py:403

commit v4 on v3

--- a/solution.py
+++ b/solution.py
@@ -41,6 +41,10 @@
     bbuf,
     peer_fin,
     peer_out,
+    guess_over,
+    rows_over,
+    go_sem,
+    ro_sem,
     in_sem,
     w_sem,
     g_sem,
@@ -92,7 +96,9 @@
     start_load(0, 1)
 
     barrier = pltpu.get_barrier_semaphore()
-    for distance in (1, 2, 3, n - 3, n - 2, n - 1):
+    forwards = n == 8
+    distances = range(1, n) if forwards else (1, 2, 3, n - 3, n - 2, n - 1)
+    for distance in distances:
         neighbour = lax.rem(me + distance, n)
         pl.semaphore_signal(
             barrier, inc=1, device_id={"layer": neighbour}, device_id_type=MESH
@@ -110,6 +116,20 @@
 
     def send_guess(q):
         return remote(gsend.at[q], shifted.at[q], g_sem.at[0, q], g_sem.at[1, q], right)
+
+    def send_guess_over():
+        return remote(gsend.at[0], guess_over, g_sem.at[0, 0], go_sem.at[0], n - 1)
+
+    def forward_guess():
+        return remote(guess_over, shifted.at[0], go_sem.at[1], g_sem.at[1, 0], 4)
+
+    def send_coarse_over(g):
+        slot = g - 1
+        return remote(bbuf.at[g], rows_over.at[slot], cs_sem.at[g], ro_sem.at[0, slot], n - 2)
+
+    def forward_coarse(g):
+        slot = g - 1
+        return remote(rows_over.at[slot], cin.at[g], ro_sem.at[1, slot], cr_sem.at[g], 4)
 
     def send_centre():
         return remote(wsend, wrecv, wx_sem.at[0], wx_sem.at[1], partner)
@@ -207,7 +227,7 @@
     def _():
         out_ref[0] = pad[1 : 1 + side, 1 : 1 + side]
 
-    pl.semaphore_wait(barrier, 6)
+    pl.semaphore_wait(barrier, len(distances))
 
     @pl.when(helps)
     def _():
@@ -223,10 +243,17 @@
 
     def emit_guess(q, value):
         gsend[q] = value
-
-        @pl.when(has_next)
+        over = (me == 3) if forwards and q == 0 else False
+
+        @pl.when(has_next & jnp.logical_not(over))
         def _():
             send_guess(q).start()
+
+        if forwards and q == 0:
+
+            @pl.when(over)
+            def _():
+                send_guess_over().start()
 
     fine(1, lambda h: wait_load(1, h), emit_guess)
 
@@ -234,6 +261,13 @@
     def _():
         for q in range(2):
             out_ref[1, :, :, :, cut(q)] = grid_of(gsend[q])
+
+    if forwards:
+
+        @pl.when(me == n - 1)
+        def _():
+            send_guess_over().wait_recv()
+            forward_guess().start()
 
     @pl.when(me >= 1)
     def _():
@@ -303,9 +337,20 @@
             second = advance(first, 1, g)
             bbuf[g] = second
 
+            over = (me == 2) if forwards and g in (1, 2) else False
+
+            @pl.when(has_next_pair & jnp.logical_not(over))
+            def _():
+                send_coarse(g).start()
+
+            if forwards and g in (1, 2):
+
+                @pl.when(over)
+                def _():
+                    send_coarse_over(g).start()
+
             @pl.when(has_next_pair)
             def _():
-                send_coarse(g).start()
                 send_fin(abuf, g).start()
                 send_out(bbuf, g).start()
 
@@ -329,6 +374,14 @@
     def _():
         force[...] = own_forcing()
         send_force().start()
+        if forwards:
+
+            @pl.when(me == n - 2)
+            def _():
+                for g in (1, 2):
+                    send_coarse_over(g).wait_recv()
+                    forward_coarse(g).start()
+
         for g in range(groups):
             send_fin(cin, g).wait_recv()
             pad[1 + g, 1 : 1 + side] = peer_fin[g]
@@ -348,6 +401,17 @@
     def _():
         for g in range(groups):
             first_coarse(g).wait_send()
+
+    if forwards:
+
+        @pl.when(me == n - 1)
+        def _():
+            forward_guess().wait_send()
+
+        @pl.when(me == n - 2)
+        def _():
+            for g in (1, 2):
+                forward_coarse(g).wait_send()
 
 
 def shards(n, images, weights, biases):
@@ -386,6 +450,10 @@
             pltpu.VMEM(piece, f32),
             pltpu.VMEM(piece, f32),
             pltpu.VMEM(piece, f32),
+            pltpu.VMEM((rows, half), f32),
+            pltpu.VMEM((2,) + piece[1:], f32),
+            pltpu.SemaphoreType.DMA((2,)),
+            pltpu.SemaphoreType.DMA((2, 2)),
             pltpu.SemaphoreType.DMA((2,)),
             pltpu.SemaphoreType.DMA((2, 2, 3)),
             pltpu.SemaphoreType.DMA((2, 2)),

time: 23.1 us -> 25.7 us (1.11)
  Pallas kernels: 21.7 us -> 24.3 us
    pallas_call x1, Pallas kernels: 21.7 us -> 24.3 us  [shards(): pl.pallas_call(functools.partial(kernel, n), out_shape=pltpu.VMEM((2, sid...]
where the time goes in v4:
time: 25.7 us; the launch traced here: 25.4 us
  Pallas kernels  24.3 us (95%)
  local copies, waits for them, and re-layouts  1.13 us (4%)
    pallas_call x1, Pallas kernels, shards(): pl.pallas_call(functools.partial(kernel, n), out_shape=pltpu.VMEM((2, sid...  24.3 us
    transpose x1, local copies, waits for them, and re-layouts, shards(): return jnp.transpose(out, (0, 3, 1, 2, 4))  1.13 us

profile of v4, /device:TPU:15, one launch (start us, length us, event | category | flops | bytes accessed | tf_op | source)
XLA Modules:
  0.0 25.4 jit_solution(6438851833032743201)
XLA Ops:
  0.0 24.3 %shard_map.37 = f32[2,4,4,8,512]{4,3,2,1,0:T(8,128)S(1)} custom-call(bf16[8,4,4,512]{3,2,1,0:T(4,128)(2,1)} %img_hbm.1, bf16[2,9,2,256,512]{4,3,2,1,0:T(8,128)(2,1)} %bitcast.3, f32[2,512]{1,0:T(2,128)} %b_hbm.1), custom_call_target="tpu_custom_call" | custom-call | tf_op jit(solution)/shard_map/pallas_call | solution.py:427
  24.3 1.1 %copy.4 = f32[2,8,4,4,512]{4,3,2,1,0:T(4,128)} copy(f32[2,8,4,4,512]{4,1,3,2,0:T(8,128)S(1)} %bitcast.2) | data formatting | bytes 1048576 | tf_op jit(solution)/shard_map/transpose | solution.py:471

commit v5 on v3

--- a/solution.py
+++ b/solution.py
@@ -40,7 +40,6 @@
     abuf,
     bbuf,
     peer_fin,
-    peer_out,
     in_sem,
     w_sem,
     g_sem,
@@ -49,7 +48,6 @@
     cs_sem,
     cr_sem,
     pf_sem,
-    po_sem,
 ):
     me = lax.axis_index("layer")
     right = lax.rem(me + 1, n)
@@ -126,9 +124,6 @@
 
     def send_fin(src, g):
         return remote(src.at[g], peer_fin.at[g], pf_sem.at[0, g], pf_sem.at[1, g], partner)
-
-    def send_out(src, g):
-        return remote(src.at[g], peer_out.at[g], po_sem.at[0, g], po_sem.at[1, g], partner)
 
     def cut(h):
         return slice(h * half, (h + 1) * half)
@@ -306,20 +301,18 @@
             @pl.when(has_next_pair)
             def _():
                 send_coarse(g).start()
-                send_fin(abuf, g).start()
-                send_out(bbuf, g).start()
-
-            @pl.when(core == 1)
-            def _():
-                send_out(abuf, g).start()
 
             pad[1 + g, 1 : 1 + side] = jnp.where(core == 0, field, first)
             out_ref[1, g] = jnp.where(core == 0, first, second)
+
+        @pl.when(has_next_pair)
+        def _():
+            for g in range(groups):
+                send_fin(abuf, g).start()
 
         fine(0, no_wait, emit_finished)
         for g in range(groups):
             send_fin(cin, g).wait_send()
-            send_out(abuf, g).wait_send()
 
             @pl.when(has_next_pair)
             def _():
@@ -333,9 +326,9 @@
             send_fin(cin, g).wait_recv()
             pad[1 + g, 1 : 1 + side] = peer_fin[g]
         fine(0, no_wait, emit_finished)
-        for g in range(groups):
-            send_out(abuf, g).wait_recv()
-            out_ref[1, g] = peer_out[g]
+        entry = peer_fin[...].reshape(rows, channels)
+        centre = wv[0, 4].reshape(channels, channels)
+        out_ref[1] = grid_of(coarse(entry, centre, b_ref[0:1, :])) + force[...]
         send_centre().wait_send()
         send_force().wait_send()
 
@@ -385,7 +378,6 @@
             pltpu.VMEM(piece, f32),
             pltpu.VMEM(piece, f32),
             pltpu.VMEM(piece, f32),
-            pltpu.VMEM(piece, f32),
             pltpu.SemaphoreType.DMA((2,)),
             pltpu.SemaphoreType.DMA((2, 2, 3)),
             pltpu.SemaphoreType.DMA((2, 2)),
@@ -394,7 +386,6 @@
             pltpu.SemaphoreType.DMA((groups,)),
             pltpu.SemaphoreType.DMA((groups,)),
             pltpu.SemaphoreType.DMA((2, groups)),
-            pltpu.SemaphoreType.DMA((2, groups)),
         ],
         compiler_params=pltpu.CompilerParams(
             collective_id=0, has_side_effects=True, vmem_limit_bytes=56 * 2**20

time: 23.1 us -> 23.1 us (level)
  no operation moved by 1% of the time
where the time goes in v5:
time: 23.1 us; the launch traced here: 22.7 us
  Pallas kernels  21.6 us (94%)
  local copies, waits for them, and re-layouts  1.13 us (5%)
    pallas_call x1, Pallas kernels, shards(): pl.pallas_call(functools.partial(kernel, n), out_shape=pltpu.VMEM((2, sid...  21.6 us
    transpose x1, local copies, waits for them, and re-layouts, shards(): return jnp.transpose(out, (0, 3, 1, 2, 4))  1.13 us

profile of v5, /device:TPU:15, one launch (start us, length us, event | category | flops | bytes accessed | tf_op | source)
XLA Modules:
  0.0 22.7 jit_solution(35353446273657056)
XLA Ops:
  0.0 21.6 %shard_map.37 = f32[2,4,4,8,512]{4,3,2,1,0:T(8,128)S(1)} custom-call(bf16[8,4,4,512]{3,2,1,0:T(4,128)(2,1)} %img_hbm.1, bf16[2,9,2,256,512]{4,3,2,1,0:T(8,128)(2,1)} %bitcast.3, f32[2,512]{1,0:T(2,128)} %b_hbm.1), custom_call_target="tpu_custom_call" | custom-call | tf_op jit(solution)/shard_map/pallas_call | solution.py:356
  21.6 1.1 %copy.4 = f32[2,8,4,4,512]{4,3,2,1,0:T(4,128)} copy(f32[2,8,4,4,512]{4,1,3,2,0:T(8,128)S(1)} %bitcast.2) | data formatting | bytes 1048576 | tf_op jit(solution)/shard_map/transpose | solution.py:394

commit v6 on v5

--- a/solution.py
+++ b/solution.py
@@ -86,8 +86,9 @@
     get_biases = pltpu.make_async_copy(b_hbm, b_ref, in_sem.at[1])
     get_images.start()
     get_biases.start()
-    start_load(0, 0)
-    start_load(0, 1)
+    for l in range(2):
+        for h in range(2):
+            start_load(l, h)
 
     barrier = pltpu.get_barrier_semaphore()
     for distance in (1, 2, 3, n - 3, n - 2, n - 1):
@@ -192,11 +193,7 @@
                     pl.ds(at, images, stride=side * tiles * side), :
                 ]
 
-    def first_layer(h):
-        wait_load(0, h)
-        start_load(1, h)
-
-    fine(0, first_layer, to_pad)
+    fine(0, lambda h: wait_load(0, h), to_pad)
 
     @pl.when(me == 0)
     def _():

time: 23.1 us -> 23.1 us (level)
  no operation moved by 1% of the time
where the time goes in v6:
time: 23.1 us; the launch traced here: 22.7 us
  Pallas kernels  21.6 us (94%)
  local copies, waits for them, and re-layouts  1.13 us (5%)
    pallas_call x1, Pallas kernels, shards(): pl.pallas_call(functools.partial(kernel, n), out_shape=pltpu.VMEM((2, sid...  21.6 us
    transpose x1, local copies, waits for them, and re-layouts, shards(): return jnp.transpose(out, (0, 3, 1, 2, 4))  1.13 us

profile of v6, /device:TPU:15, one launch (start us, length us, event | category | flops | bytes accessed | tf_op | source)
XLA Modules:
  0.0 22.7 jit_solution(8760488659105062642)
XLA Ops:
  0.0 21.6 %shard_map.37 = f32[2,4,4,8,512]{4,3,2,1,0:T(8,128)S(1)} custom-call(bf16[8,4,4,512]{3,2,1,0:T(4,128)(2,1)} %img_hbm.1, bf16[2,9,2,256,512]{4,3,2,1,0:T(8,128)(2,1)} %bitcast.3, f32[2,512]{1,0:T(2,128)} %b_hbm.1), custom_call_target="tpu_custom_call" | custom-call | tf_op jit(solution)/shard_map/pallas_call | solution.py:353
  21.6 1.1 %copy.4 = f32[2,8,4,4,512]{4,3,2,1,0:T(4,128)} copy(f32[2,8,4,4,512]{4,1,3,2,0:T(8,128)S(1)} %bitcast.2) | data formatting | bytes 1048576 | tf_op jit(solution)/shard_map/transpose | solution.py:391

commit v7 on v6

--- a/solution.py
+++ b/solution.py
@@ -278,29 +278,32 @@
         send_force().wait_recv()
 
         def advance(field, b, g):
-            flat = field.reshape(side * images, channels)
+            flat = field.reshape(2 * side * images, channels)
             solved = coarse(flat, wc[b], bc[b, 0:1, :])
-            return solved.reshape(side, images, channels) + fo[b, g]
-
-        for g in range(groups):
-            send_coarse(g).wait_recv()
+            return solved.reshape(2, side, images, channels) + fo[b, g : g + 2]
+
+        for g in range(0, groups, 2):
+            for r in (g, g + 1):
+                send_coarse(r).wait_recv()
 
             @pl.when(core == 1)
             def _():
-                send_fin(cin, g).start()
-
-            field = cin[g]
+                for r in (g, g + 1):
+                    send_fin(cin, r).start()
+
+            field = cin[g : g + 2]
             first = advance(field, 0, g)
-            abuf[g] = first
+            abuf[g : g + 2] = first
             second = advance(first, 1, g)
-            bbuf[g] = second
+            bbuf[g : g + 2] = second
 
             @pl.when(has_next_pair)
             def _():
-                send_coarse(g).start()
-
-            pad[1 + g, 1 : 1 + side] = jnp.where(core == 0, field, first)
-            out_ref[1, g] = jnp.where(core == 0, first, second)
+                for r in (g, g + 1):
+                    send_coarse(r).start()
+
+            pad[1 + g : 3 + g, 1 : 1 + side] = jnp.where(core == 0, field, first)
+            out_ref[1, g : g + 2] = jnp.where(core == 0, first, second)
 
         @pl.when(has_next_pair)
         def _():

time: 23.1 us -> 24.3 us (1.052)
  Pallas kernels: 21.6 us -> 22.8 us
    pallas_call x1, Pallas kernels: 21.6 us -> 22.8 us  [shards(): pl.pallas_call(functools.partial(kernel, n), out_shape=pltpu.VMEM((2, sid...]
where the time goes in v7:
time: 24.3 us; the launch traced here: 23.9 us
  Pallas kernels  22.8 us (94%)
  local copies, waits for them, and re-layouts  1.13 us (5%)
    pallas_call x1, Pallas kernels, shards(): pl.pallas_call(functools.partial(kernel, n), out_shape=pltpu.VMEM((2, sid...  22.8 us
    transpose x1, local copies, waits for them, and re-layouts, shards(): return jnp.transpose(out, (0, 3, 1, 2, 4))  1.13 us

profile of v7, /device:TPU:15, one launch (start us, length us, event | category | flops | bytes accessed | tf_op | source)
XLA Modules:
  0.0 23.9 jit_solution(13464955651682591022)
XLA Ops:
  0.0 22.8 %shard_map.37 = f32[2,4,4,8,512]{4,3,2,1,0:T(8,128)S(1)} custom-call(bf16[8,4,4,512]{3,2,1,0:T(4,128)(2,1)} %img_hbm.1, bf16[2,9,2,256,512]{4,3,2,1,0:T(8,128)(2,1)} %bitcast.3, f32[2,512]{1,0:T(2,128)} %b_hbm.1), custom_call_target="tpu_custom_call" | custom-call | tf_op jit(solution)/shard_map/pallas_call | solution.py:356
  22.8 1.1 %copy.4 = f32[2,8,4,4,512]{4,3,2,1,0:T(4,128)} copy(f32[2,8,4,4,512]{4,1,3,2,0:T(8,128)S(1)} %bitcast.2) | data formatting | bytes 1048576 | tf_op jit(solution)/shard_map/transpose | solution.py:394
